TPU v7x, 256 devices: a whole 4x4x8 slice. The times are simulated.
256 devices in a mesh: row: 16 (over z, core), col: 16 (over x, y).
Axes of the slice: x: 4, y: 4, z: 8, core: 2. Of those that a mesh axis runs over, the one named last changes fastest.
Arguments:
- tokens: bfloat16 [2048, 6144], P('col', 'row'), may hold values from -6 to 6
- w_in: bfloat16 [6144, 24576], P('row', 'col'), may hold values from -0.078125 to 0.078125
- w_out: bfloat16 [24576, 6144], P('col', 'row'), may hold values from -0.0390625 to 0.0390625
- cotangent: bfloat16 [2048, 6144], P('col', 'row'), may hold values from -6 to 6
Outputs:
- mixed: bfloat16 [2048, 6144], P('col', 'row')
- grad_tokens: bfloat16 [2048, 6144], P('col', 'row')
- grad_w_in: float32 [6144, 24576], P('row', 'col')
- grad_w_out: float32 [24576, 6144], P('col', 'row')
All inputs are finite; a program needn't handle non-finite values.
Results may differ from a plain program's by a relative error of at most 0.033.
Values may be sent and summed in bfloat16 or wider, within the bound.
No kernel may reach another device: no remote copies, remote signals or barrier semaphores. Data moves between devices by JAX's collectives and lax.ppermute only.
A program may use at most 128 MiB of HBM per device.

v0:
```python
import math

import jax
import jax.numpy as jnp
from jax import lax
from jax.sharding import PartitionSpec as P


def gelu_value(v):
    return v * 0.5 * (1.0 + lax.erf(v / math.sqrt(2.0)))


def gelu_slope(v):
    return 0.5 * (1.0 + lax.erf(v / math.sqrt(2.0))) + v * jnp.exp(-0.5 * v * v) / math.sqrt(
        2.0 * math.pi
    )


def on_device(tokens, w_in, w_out, cotangent):
    contract_rows = (((0,), (0,)), ((), ()))
    contract_cols = (((1,), (1,)), ((), ()))
    x_all = lax.all_gather(tokens, "col", axis=0, tiled=True)
    block = x_all
    pre = lax.psum_scatter(
        jnp.dot(block, w_in, preferred_element_type=jnp.float32).astype(jnp.bfloat16),
        "row",
        scatter_dimension=0,
        tiled=True,
    ).astype(jnp.float32)
    dy_all = lax.all_gather(cotangent, "col", axis=0, tiled=True)
    block = dy_all
    grad_hidden = lax.psum_scatter(
        lax.dot_general(block, w_out, contract_cols, preferred_element_type=jnp.float32).astype(
            jnp.bfloat16
        ),
        "row",
        scatter_dimension=0,
        tiled=True,
    ).astype(jnp.float32)
    hidden = gelu_value(pre).astype(jnp.bfloat16)
    h_all = lax.all_gather(hidden, "row", axis=0, tiled=True)
    block = h_all
    mixed = lax.psum_scatter(
        jnp.dot(block, w_out, preferred_element_type=jnp.float32).astype(jnp.bfloat16),
        "col",
        scatter_dimension=0,
        tiled=True,
    )
    grad_pre = (grad_hidden * gelu_slope(pre)).astype(jnp.bfloat16)
    dg_all = lax.all_gather(grad_pre, "row", axis=0, tiled=True)
    block = dg_all
    grad_tokens = lax.psum_scatter(
        lax.dot_general(block, w_in, contract_cols, preferred_element_type=jnp.float32).astype(
            jnp.bfloat16
        ),
        "col",
        scatter_dimension=0,
        tiled=True,
    )
    factor = 1.0 / math.sqrt(x_all.shape[0])
    grad_w_in = (
        lax.dot_general(x_all, dg_all, contract_rows, preferred_element_type=jnp.float32) * factor
    )
    grad_w_out = (
        lax.dot_general(h_all, dy_all, contract_rows, preferred_element_type=jnp.float32) * factor
    )
    return (mixed, grad_tokens, grad_w_in, grad_w_out)


def solution(mesh):
    placed = (P("col", "row"), P("row", "col"), P("col", "row"), P("col", "row"))
    return jax.shard_map(
        on_device,
        mesh=mesh,
        in_specs=placed,
        out_specs=(P("col", "row"), P("col", "row"), P("row", "col"), P("col", "row")),
        check_vma=False,
    )
```

profile of v0, /device:TPU:1, one launch (start us, length us, event | category | flops | bytes accessed | tf_op | source)
XLA Modules:
  0.0 513.3 jit_solution(17314910928026412725)
XLA Ops:
  7.2 0.7 all-gather.9.cloned.1.call-update
  8.0 0.7 all-gather.5.cloned.1.call-update
  8.7 0.0 reduce-scatter.9.cloned.1.call-start
  8.7 53.6 %all-gather.9.cloned.1.call-done = bf16[2048,384]{1,0:T(8,128)(2,1)} async-done(((bf16[128,384]{1,0:T(8,128)(2,1)}), bf16[2048,384]{1,0:T(8,128)(2,1)}) %all-gather.9.cloned.1.call-update) | async-done | bytes 1572880 | tf_op jit(solution)/shard_map/all_gather | solution.py:30
  62.3 6.8 %convolution_convert_fusion = bf16[2048,1536]{1,0:T(8,128)(2,1)} fusion(bf16[2048,384]{1,0:T(8,128)(2,1)} %all-gather.9.cloned.1.call-done, bf16[1536,384]{1,0:T(8,128)(2,1)S(1)} %copy-done), kind=kOutput, calls=%fused_computation | convolution fusion | flops 2419064832 | bytes 9043968 | tf_op jit(solution)/shard_map/dot_general | solution.py:33
  69.2 0.0 reduce-scatter.5.cloned.1.call-start
  69.2 44.0 %all-gather.5.cloned.1.call-done = bf16[2048,384]{1,0:T(8,128)(2,1)} async-done(((bf16[128,384]{1,0:T(8,128)(2,1)}), bf16[2048,384]{1,0:T(8,128)(2,1)}) %all-gather.5.cloned.1.call-update) | async-done | bytes 1572880 | tf_op jit(solution)/shard_map/all_gather | solution.py:22
  113.2 6.7 %convolution_convert_fusion.1 = bf16[2048,1536]{1,0:T(8,128)(2,1)} fusion(bf16[2048,384]{1,0:T(8,128)(2,1)} %all-gather.5.cloned.1.call-done, bf16[384,1536]{1,0:T(8,128)(2,1)S(1)} %copy-done.1), kind=kOutput, calls=%fused_computation.1 | convolution fusion | flops 2419064832 | bytes 9043968 | tf_op jit(solution)/shard_map/dot_general | solution.py:25
  119.9 0.0 all-gather.7.cloned.1.call-start
  120.0 59.7 %reduce-scatter.9.cloned.1.call-done = bf16[128,1536]{1,0:T(8,128)(2,1)} async-done(((bf16[2048,1536]{1,0:T(8,128)(2,1)}), bf16[128,1536]{1,0:T(8,128)(2,1)}) %reduce-scatter.9.cloned.1.call-update) | async-done | bytes 393232 | tf_op jit(solution)/shard_map/reduce_scatter | solution.py:32
  179.7 67.7 %reduce-scatter.5.cloned.1.call-done = bf16[128,1536]{1,0:T(8,128)(2,1)} async-done(((bf16[2048,1536]{1,0:T(8,128)(2,1)}), bf16[128,1536]{1,0:T(8,128)(2,1)}) %reduce-scatter.5.cloned.1.call-update) | async-done | bytes 393232 | tf_op jit(solution)/shard_map/reduce_scatter | solution.py:24
  247.3 2.4 fusion.9
  249.8 0.0 all-gather.11.cloned.1.call-start
  249.8 0.5 all-gather.11.cloned.1.call-update
  250.4 47.7 %all-gather.7.cloned.1.call-done = bf16[2048,1536]{1,0:T(8,128)(2,1)} async-done(((bf16[128,1536]{1,0:T(8,128)(2,1)}), bf16[2048,1536]{1,0:T(8,128)(2,1)}) %all-gather.7.cloned.1.call-update) | async-done | bytes 6291472 | tf_op jit(solution)/shard_map/all_gather | solution.py:41
  298.1 7.4 %convolution_convert_fusion.3 = bf16[2048,384]{1,0:T(8,128)(2,1)} fusion(bf16[2048,1536]{1,0:T(8,128)(2,1)} %all-gather.7.cloned.1.call-done, bf16[1536,384]{1,0:T(8,128)(2,1)S(1)} %copy-done), kind=kOutput, calls=%fused_computation.6 | convolution fusion | flops 2416705536 | bytes 9043968 | tf_op jit(solution)/shard_map/dot_general | solution.py:44
  305.5 0.2 reduce-scatter.11.cloned.1.call-start
  305.7 39.4 %all-gather.11.cloned.1.call-done = bf16[2048,1536]{1,0:T(8,128)(2,1)} async-done(((bf16[128,1536]{1,0:T(8,128)(2,1)}), bf16[2048,1536]{1,0:T(8,128)(2,1)}) %all-gather.11.cloned.1.call-update) | async-done | bytes 6291472 | tf_op jit(solution)/shard_map/all_gather | solution.py:50
  345.1 7.4 %convolution_convert_fusion.2 = bf16[2048,384]{1,0:T(8,128)(2,1)} fusion(bf16[2048,1536]{1,0:T(8,128)(2,1)} %all-gather.11.cloned.1.call-done, bf16[384,1536]{1,0:T(8,128)(2,1)S(1)} %copy-done.1), kind=kOutput, calls=%fused_computation.5 | convolution fusion | flops 2416705536 | bytes 9043968 | tf_op jit(solution)/shard_map/dot_general | solution.py:53
  352.5 6.0 %fusion = f32[384,1536]{0,1:T(8,128)S(1)} fusion(bf16[2048,1536]{1,0:T(8,128)(2,1)} %all-gather.11.cloned.1.call-done, bf16[2048,384]{1,0:T(8,128)(2,1)} %all-gather.5.cloned.1.call-done), kind=kOutput, calls=%fused_computation.4 | convolution fusion | flops 2416508928 | bytes 10223616 | tf_op jit(solution)/shard_map/dot_general | solution.py:62
  358.5 2.0 copy.8
  360.5 8.1 %convolution_multiply_fusion = f32[1536,384]{1,0:T(8,128)} fusion(bf16[2048,1536]{1,0:T(8,128)(2,1)} %all-gather.7.cloned.1.call-done, bf16[2048,384]{1,0:T(8,128)(2,1)} %all-gather.9.cloned.1.call-done), kind=kOutput, calls=%fused_computation.2 | convolution fusion | flops 2416508928 | bytes 10223616 | tf_op jit(solution)/shard_map/dot_general | solution.py:65
  368.6 55.9 %reduce-scatter.7.cloned.1.call-done = bf16[128,384]{1,0:T(8,128)(2,1)} async-done(((bf16[2048,384]{1,0:T(8,128)(2,1)}), bf16[128,384]{1,0:T(8,128)(2,1)}) %reduce-scatter.7.cloned.1.call-update) | async-done | bytes 98320 | tf_op jit(solution)/shard_map/reduce_scatter | solution.py:43
  424.4 82.0 %reduce-scatter.11.cloned.1.call-done = bf16[128,384]{1,0:T(8,128)(2,1)} async-done(((bf16[2048,384]{1,0:T(8,128)(2,1)}), bf16[128,384]{1,0:T(8,128)(2,1)}) %reduce-scatter.11.cloned.1.call-update) | async-done | bytes 98320 | tf_op jit(solution)/shard_map/reduce_scatter | solution.py:52
  (12 shorter events, 0.2 us)
Async XLA Ops:
  7.2 55.2 %copy-start = (bf16[1536,384]{1,0:T(8,128)(2,1)S(1)}, bf16[1536,384]{1,0:T(8,128)(2,1)}, u32[]{:S(2)}) copy-start(bf16[1536,384]{1,0:T(8,128)(2,1)} %param.6) | copy-start | bytes 3538948
  7.2 55.2 %all-gather.9.cloned.1.call-start = ((), (), s32[]{:S(2)}) async-start(), calls=%async_computation.8 | async-start | bytes 1671168 | tf_op jit(solution)/shard_map/all_gather | solution.py:30
  7.9 105.3 %all-gather.5.cloned.1.call-start = ((), (), s32[]{:S(2)}) async-start(), calls=%async_computation.4 | async-start | bytes 1671168 | tf_op jit(solution)/shard_map/all_gather | solution.py:22
  8.7 171.0 %reduce-scatter.9.cloned.1.call-start = ((), (), s32[]{:S(2)}) async-start(), calls=%async_computation.9 | async-start | bytes 6684672 | tf_op jit(solution)/shard_map/reduce_scatter | solution.py:32
  69.2 44.1 %copy-start.1 = (bf16[384,1536]{1,0:T(8,128)(2,1)S(1)}, bf16[384,1536]{1,0:T(8,128)(2,1)}, u32[]{:S(2)}) copy-start(bf16[384,1536]{1,0:T(8,128)(2,1)} %param.5) | copy-start | bytes 3538948
  69.2 178.1 %reduce-scatter.5.cloned.1.call-start = ((), (), s32[]{:S(2)}) async-start(), calls=%async_computation.5 | async-start | bytes 6684672 | tf_op jit(solution)/shard_map/reduce_scatter | solution.py:24
  119.9 178.2 %all-gather.7.cloned.1.call-start = ((), (), s32[]{:S(2)}) async-start(), calls=%async_computation.6 | async-start | bytes 6684672 | tf_op jit(solution)/shard_map/all_gather | solution.py:41
  249.8 95.3 %all-gather.11.cloned.1.call-start = ((), (), s32[]{:S(2)}) async-start(), calls=%async_computation.10 | async-start | bytes 6684672 | tf_op jit(solution)/shard_map/all_gather | solution.py:50
  250.4 174.1 %reduce-scatter.7.cloned.1.call-start = ((), (), s32[]{:S(2)}) async-start(), calls=%async_computation.7 | async-start | bytes 1671168 | tf_op jit(solution)/shard_map/reduce_scatter | solution.py:43
  305.5 201.0 %reduce-scatter.11.cloned.1.call-start = ((), (), s32[]{:S(2)}) async-start(), calls=%async_computation.11 | async-start | bytes 1671168 | tf_op jit(solution)/shard_map/reduce_scatter | solution.py:52
Sparse Core Ops, SparseCore 0:
  10.5 51.7 all-gather.8
  64.8 48.3 all-gather.4
  115.8 63.8 reduce-scatter.8
  182.1 65.2 reduce-scatter.4
  249.9 48.1 all-gather.6
  300.4 44.6 all-gather.10
  349.2 75.2 reduce-scatter.6
  428.5 77.9 reduce-scatter.10
where the time goes:
time: 514 us; the launch traced here: 513 us
  waiting for transfers between devices  452 us (88%)
  matrix products  42.4 us (8%)
  between operations  14.2 us (3%)
    reduce_scatter x1, waiting for transfers between devices, on_device(): lax.psum_scatter(lax.dot_general(block, w_in, contract_cols, preferred_el...  82 us
    reduce_scatter x1, waiting for transfers between devices, on_device(): lax.psum_scatter(jnp.dot(block, w_in, preferred_element_type=jnp.float32)...  67.7 us
    reduce_scatter x1, waiting for transfers between devices, on_device(): lax.psum_scatter(lax.dot_general(block, w_out, contract_cols, preferred_e...  59.7 us
    reduce_scatter x1, waiting for transfers between devices, on_device(): lax.psum_scatter(jnp.dot(block, w_out, preferred_element_type=jnp.float32...  55.9 us
    all_gather x1, waiting for transfers between devices, on_device(): dy_all = lax.all_gather(cotangent, 'col', axis=0, tiled=True)  53.6 us
    all_gather x1, waiting for transfers between devices, on_device(): h_all = lax.all_gather(hidden, 'row', axis=0, tiled=True)  47.7 us
    all_gather x1, waiting for transfers between devices, on_device(): x_all = lax.all_gather(tokens, 'col', axis=0, tiled=True)  44 us
    all_gather x1, waiting for transfers between devices, on_device(): dg_all = lax.all_gather(grad_pre, 'row', axis=0, tiled=True)  39.4 us
  transfers between devices with their start and end apart: 8, of which 8 were waited for; matrix products, arithmetic and copies ran while one was open for 9% of the time, Pallas kernels for 0%

commit v1 on v0

v1 whole, which is shorter than its diff:
```python
import math

import jax
import jax.numpy as jnp
from jax import lax
from jax.sharding import PartitionSpec as P

BF = jnp.bfloat16
F32 = jnp.float32
ROWS, COLS = 16, 16
SWAP = [(r, r ^ 1) for r in range(ROWS)]
SAME_CORE = [[2 * z + k for z in range(ROWS // 2)] for k in range(2)]
CONTRACT_ROWS = (((0,), (0,)), ((), ()))
CONTRACT_COLS = (((1,), (1,)), ((), ()))


def gelu_value(v):
    return v * 0.5 * (1.0 + lax.erf(v / math.sqrt(2.0)))


def gelu_slope(v):
    return 0.5 * (1.0 + lax.erf(v / math.sqrt(2.0))) + v * jnp.exp(-0.5 * v * v) / math.sqrt(
        2.0 * math.pi
    )


def swap(a):
    return lax.ppermute(a, "row", SWAP)


def gather_tokens(a, core):
    half = a.shape[0] // 2
    mine = lax.dynamic_slice_in_dim(a, core * half, half, 0)
    others = swap(lax.dynamic_slice_in_dim(a, (1 - core) * half, half, 0))
    block = jnp.concatenate([mine, others], axis=1)
    every = lax.all_to_all(jnp.broadcast_to(block[None], (COLS,) + block.shape), "col", 0, 0)
    return every.reshape(COLS * half, block.shape[1])


def scatter_tokens(a, core):
    half = a.shape[0] // COLS
    width = a.shape[1] // 2
    parts = lax.all_to_all(a.reshape(COLS, half, a.shape[1]), "col", 0, 0)
    total = jnp.sum(parts.astype(F32), axis=0).astype(BF)
    others = swap(total[:, width:])
    mine = total[:, :width]
    first = core == 0
    return jnp.concatenate([jnp.where(first, mine, others), jnp.where(first, others, mine)], axis=0)


def scatter_rows(a):
    return lax.psum_scatter(
        a, "row", scatter_dimension=0, axis_index_groups=SAME_CORE, tiled=True
    ).astype(F32)


def gather_rows(a):
    return lax.all_gather(a, "row", axis=0, axis_index_groups=SAME_CORE, tiled=True)


def on_device(tokens, w_in, w_out, cotangent):
    core = lax.rem(lax.axis_index("row"), 2)
    width = w_in.shape[0]
    x_all = gather_tokens(tokens, core)
    w_in2 = jnp.concatenate([w_in, swap(w_in)], axis=0)
    pre = scatter_rows(jnp.dot(x_all, w_in2, preferred_element_type=F32).astype(BF))
    dy_all = gather_tokens(cotangent, core)
    w_out2 = jnp.concatenate([w_out, swap(w_out)], axis=1)
    grad_hidden = scatter_rows(
        lax.dot_general(dy_all, w_out2, CONTRACT_COLS, preferred_element_type=F32).astype(BF)
    )
    hidden = gelu_value(pre).astype(BF)
    h_all = gather_rows(hidden)
    mixed = scatter_tokens(jnp.dot(h_all, w_out2, preferred_element_type=F32).astype(BF), core)
    grad_pre = (grad_hidden * gelu_slope(pre)).astype(BF)
    dg_all = gather_rows(grad_pre)
    grad_tokens = scatter_tokens(
        lax.dot_general(dg_all, w_in2, CONTRACT_COLS, preferred_element_type=F32).astype(BF), core
    )
    factor = 1.0 / math.sqrt(COLS * tokens.shape[0])
    half_in = lax.dot_general(x_all, dg_all, CONTRACT_ROWS, preferred_element_type=F32)
    grad_w_in = (half_in[:width] + swap(half_in[width:].astype(BF)).astype(F32)) * factor
    half_out = lax.dot_general(h_all, dy_all, CONTRACT_ROWS, preferred_element_type=F32)
    grad_w_out = (half_out[:, :width] + swap(half_out[:, width:].astype(BF)).astype(F32)) * factor
    return (mixed, grad_tokens, grad_w_in, grad_w_out)


def solution(mesh):
    placed = (P("col", "row"), P("row", "col"), P("col", "row"), P("col", "row"))
    return jax.shard_map(
        on_device,
        mesh=mesh,
        in_specs=placed,
        out_specs=(P("col", "row"), P("col", "row"), P("row", "col"), P("col", "row")),
        check_vma=False,
    )
```

time: 514 us -> 294 us (0.57)
  waiting for transfers between devices: 452 us -> 187 us
  starting transfers between devices: 0.5 us -> 36.6 us
  local copies, waits for them, and re-layouts: 1.96 us -> 13.3 us
  matrix products: 42.4 us -> 31.2 us
  other arithmetic: 2.42 us -> 11.7 us
    reduce_scatter x4 -> x2, waiting for transfers between devices: 265 us -> 54.9 us  [scatter_rows(): lax.psum_scatter(a, 'row', scatter_dimension=0, axis_index_groups=SAME_CO...]
    all_gather x4 -> x2, waiting for transfers between devices: 185 us -> 78.7 us  [gather_rows(): lax.all_gather(a, 'row', axis=0, axis_index_groups=SAME_CORE, tiled=True)]
    all_to_all x0 -> x4, waiting for transfers between devices: none -> 48.9 us  [the longest x2 37.3 us: gather_tokens(): lax.all_to_all(jnp.broadcast_to(block[None], (COLS,) + block.shape), 'col...]
    all_to_all x0 -> x4, starting transfers between devices: none -> 21.8 us  [the longest x2 13.1 us: scatter_tokens(): parts = lax.all_to_all(a.reshape(COLS, half, a.shape[1]), 'col', 0, 0)]
    ppermute x0 -> x8, starting transfers between devices: none -> 14.6 us  [swap(): return lax.ppermute(a, 'row', SWAP)]
    dot_general x6, matrix products: 42.4 us -> 31.2 us  [the longest x1 6.37 us: on_device(): jnp.dot(h_all, w_out2, preferred_element_type=F32).astype(BF)]
    mul x0 -> x2, other arithmetic: none -> 7.44 us  [the longest x1 3.78 us: on_device(): (half_in[:width] + swap(half_in[width:].astype(BF)).astype(F32)) * factor]
  transfers between devices with their start and end apart: 8 -> 16, of which waited for: 8 -> 12; matrix products, arithmetic and copies ran while one was open for 9% -> 15% of each run, Pallas kernels for 0% -> 0%
where the time goes in v1:
time: 294 us; the launch traced here: 293 us
  waiting for transfers between devices  187 us (64%)
  starting transfers between devices  36.6 us (12%)
  matrix products  31.2 us (11%)
  between operations  13.9 us (5%)
  local copies, waits for them, and re-layouts  13.3 us (5%)
  other arithmetic  11.7 us (4%)
    all_gather x2, waiting for transfers between devices, gather_rows(): lax.all_gather(a, 'row', axis=0, axis_index_groups=SAME_CORE, tiled=True)  78.7 us
    reduce_scatter x2, waiting for transfers between devices, scatter_rows(): lax.psum_scatter(a, 'row', scatter_dimension=0, axis_index_groups=SAME_CO...  54.9 us
    all_to_all x2, waiting for transfers between devices, gather_tokens(): lax.all_to_all(jnp.broadcast_to(block[None], (COLS,) + block.shape), 'col...  37.3 us
    ppermute x8, starting transfers between devices, swap(): return lax.ppermute(a, 'row', SWAP)  14.6 us
    all_to_all x2, starting transfers between devices, scatter_tokens(): parts = lax.all_to_all(a.reshape(COLS, half, a.shape[1]), 'col', 0, 0)  13.1 us
    all_to_all x2, waiting for transfers between devices, scatter_tokens(): parts = lax.all_to_all(a.reshape(COLS, half, a.shape[1]), 'col', 0, 0)  11.6 us
    all_to_all x2, starting transfers between devices, gather_tokens(): lax.all_to_all(jnp.broadcast_to(block[None], (COLS,) + block.shape), 'col...  8.73 us
    dot_general x1, matrix products, on_device(): jnp.dot(h_all, w_out2, preferred_element_type=F32).astype(BF)  6.37 us
  transfers between devices with their start and end apart: 16, of which 12 were waited for; matrix products, arithmetic and copies ran while one was open for 15% of the time, Pallas kernels for 0%

profile of v1, /device:TPU:1, one launch (start us, length us, event | category | flops | bytes accessed | tf_op | source)
XLA Modules:
  0.0 293.5 jit_solution(15160826024839561457)
XLA Ops:
  8.0 3.3 %collective-permute-start = (bf16[64,384]{1,0:T(8,128)(2,1)S(1)}, bf16[64,384]{1,0:T(8,128)(2,1)S(1)}, u32[]{:S(2)}, u32[]{:S(2)}) collective-permute-start(bf16[64,384]{1,0:T(8,128)(2,1)S(1)} %get-tuple-element.13), channel_id=1, source_target_pairs={{0,16},{16,0},{32,48},{48,32},{64,80},{80,64},{96,112},{112,96},{1... | collective-permute-start | bytes 147464 | tf_op jit(solution)/shard_map/ppermute | solution.py:28
  13.6 5.0 %all-to-all-start = ((bf16[16,64,768]{2,1,0:T(8,128)(2,1)}), bf16[16,64,768]{2,1,0:T(8,128)(2,1)S(1)}, u32[]{:S(2)}, u32[]{:S(2)}) async-start(bf16[16,64,768]{2,1,0:T(8,128)(2,1)} %broadcast_in_dim.4), calls=%async_computation | async-start | bytes 3145728 | tf_op jit(solution)/shard_map/all_to_all | solution.py:36
  22.9 18.0 %all-to-all-done = bf16[16,64,768]{2,1,0:T(8,128)(2,1)S(1)} async-done(((bf16[16,64,768]{2,1,0:T(8,128)(2,1)}), bf16[16,64,768]{2,1,0:T(8,128)(2,1)S(1)}, u32[]{:S(2)}, u32[]{:S(2)}) %all-to-all-start) | async-done | bytes 1572896 | tf_op jit(solution)/shard_map/all_to_all | solution.py:36
  41.0 5.6 %convolution_convert_fusion.1 = bf16[1024,1536]{1,0:T(8,128)(2,1)} fusion(bf16[1024,768]{1,0:T(8,128)(2,1)S(1)} %bitcast.16, bf16[768,1536]{1,0:T(8,128)(2,1)} %constant_dynamic-update-slice_fusion), kind=kOutput, calls=%fused_computation.1 | convolution fusion | flops 2417491968 | bytes 7077888 | tf_op jit(solution)/shard_map/dot_general | solution.py:66
  47.5 2.7 collective-permute-start.4
  52.4 3.7 %all-to-all-start.2 = ((bf16[16,64,768]{2,1,0:T(8,128)(2,1)}), bf16[16,64,768]{2,1,0:T(8,128)(2,1)S(1)}, u32[]{:S(2)}, u32[]{:S(2)}) async-start(bf16[16,64,768]{2,1,0:T(8,128)(2,1)} %broadcast_in_dim.5), calls=%async_computation.3 | async-start | bytes 3145728 | tf_op jit(solution)/shard_map/all_to_all | solution.py:36
  56.6 2.4 constant_dynamic-update-slice_fusion.3
  60.5 19.3 %all-to-all-done.2 = bf16[16,64,768]{2,1,0:T(8,128)(2,1)S(1)} async-done(((bf16[16,64,768]{2,1,0:T(8,128)(2,1)}), bf16[16,64,768]{2,1,0:T(8,128)(2,1)S(1)}, u32[]{:S(2)}, u32[]{:S(2)}) %all-to-all-start.2) | async-done | bytes 1572896 | tf_op jit(solution)/shard_map/all_to_all | solution.py:36
  79.8 6.3 %convolution_convert_fusion = bf16[1024,1536]{1,0:T(8,128)(2,1)} fusion(bf16[1024,768]{1,0:T(8,128)(2,1)S(1)} %bitcast.18, bf16[1536,768]{1,0:T(8,128)(2,1)} %constant_dynamic-update-slice_fusion.2), kind=kOutput, calls=%fused_computation | convolution fusion | flops 2417491968 | bytes 7077888 | tf_op jit(solution)/shard_map/dot_general | solution.py:70
  86.2 6.2 %reduce-scatter.3.cloned.1.call-done = bf16[128,1536]{1,0:T(8,128)(2,1)} async-done(((bf16[1024,1536]{1,0:T(8,128)(2,1)}), bf16[128,1536]{1,0:T(8,128)(2,1)}) %reduce-scatter.3.cloned.1.call-update) | async-done | bytes 393232 | tf_op jit(solution)/shard_map/reduce_scatter | solution.py:52
  92.4 48.7 %reduce-scatter.5.cloned.1.call-done = bf16[128,1536]{1,0:T(8,128)(2,1)} async-done(((bf16[1024,1536]{1,0:T(8,128)(2,1)}), bf16[128,1536]{1,0:T(8,128)(2,1)}) %reduce-scatter.5.cloned.1.call-update) | async-done | bytes 393232 | tf_op jit(solution)/shard_map/reduce_scatter | solution.py:52
  141.1 2.4 fusion.10
  144.1 46.4 %all-gather.3.cloned.1.call-done = bf16[1024,1536]{1,0:T(8,128)(2,1)} async-done(((bf16[128,1536]{1,0:T(8,128)(2,1)}), bf16[1024,1536]{1,0:T(8,128)(2,1)}) %all-gather.3.cloned.1.call-update) | async-done | bytes 3145744 | tf_op jit(solution)/shard_map/all_gather | solution.py:58
  190.5 6.4 %convolution_convert_fusion.3 = bf16[1024,768]{1,0:T(8,128)(2,1)} fusion(bf16[1024,1536]{1,0:T(8,128)(2,1)} %all-gather.3.cloned.1.call-done, bf16[1536,768]{1,0:T(8,128)(2,1)} %constant_dynamic-update-slice_fusion.2), kind=kOutput, calls=%fused_computation.9 | convolution fusion | flops 2416705536 | bytes 7077888 | tf_op jit(solution)/shard_map/dot_general | solution.py:74
  196.9 6.5 %all-to-all-start.1 = ((bf16[16,64,768]{2,1,0:T(8,128)(2,1)}), bf16[16,64,768]{2,1,0:T(8,128)(2,1)S(1)}, u32[]{:S(2)}, u32[]{:S(2)}) async-start(bf16[16,64,768]{2,1,0:T(8,128)(2,1)} %bitcast.21), calls=%async_computation.2 | async-start | bytes 3145728 | tf_op jit(solution)/shard_map/all_to_all | solution.py:43
  203.4 32.4 %all-gather.5.cloned.1.call-done = bf16[1024,1536]{1,0:T(8,128)(2,1)} async-done(((bf16[128,1536]{1,0:T(8,128)(2,1)}), bf16[1024,1536]{1,0:T(8,128)(2,1)}) %all-gather.5.cloned.1.call-update) | async-done | bytes 3145744 | tf_op jit(solution)/shard_map/all_gather | solution.py:58
  235.8 4.7 %fusion.11 = f32[768,1536]{1,0:T(8,128)S(1)} fusion(bf16[1024,768]{1,0:T(8,128)(2,1)S(1)} %bitcast.17, bf16[1024,1536]{1,0:T(8,128)(2,1)} %all-gather.5.cloned.1.call-done), kind=kOutput, calls=%fused_computation.40 | convolution fusion | flops 2415919104 | bytes 9437184 | tf_op jit(solution)/shard_map/dot_general | solution.py:81
  243.0 2.8 fusion.12
  248.3 5.4 %convolution_convert_fusion.2 = bf16[1024,768]{1,0:T(8,128)(2,1)} fusion(bf16[1024,1536]{1,0:T(8,128)(2,1)S(1)} %copy-done.1, bf16[768,1536]{1,0:T(8,128)(2,1)} %constant_dynamic-update-slice_fusion), kind=kOutput, calls=%fused_computation.8 | convolution fusion | flops 2416705536 | bytes 7077888 | tf_op jit(solution)/shard_map/dot_general | solution.py:78
  253.8 6.5 %all-to-all-start.3 = ((bf16[16,64,768]{2,1,0:T(8,128)(2,1)}), bf16[16,64,768]{2,1,0:T(8,128)(2,1)S(1)}, u32[]{:S(2)}, u32[]{:S(2)}) async-start(bf16[16,64,768]{2,1,0:T(8,128)(2,1)} %bitcast.20), calls=%async_computation.5 | async-start | bytes 3145728 | tf_op jit(solution)/shard_map/all_to_all | solution.py:43
  260.3 3.8 %fusion.1 = f32[384,1536]{1,0:T(8,128)} fusion(f32[768,1536]{1,0:T(8,128)} %copy-done, bf16[384,1536]{1,0:T(8,128)(2,1)} %collective-permute-done.6), kind=kLoop, calls=%fused_computation.7 | loop fusion | flops 1769472 | bytes 5898240 | tf_op jit(solution)/shard_map/mul | solution.py:82
  265.6 3.7 %fusion = f32[1536,384]{1,0:T(8,128)} fusion(f32[1536,768]{1,0:T(8,128)} %copy-done.2, bf16[1536,384]{1,0:T(8,128)(2,1)} %collective-permute-done.7), kind=kLoop, calls=%fused_computation.4 | loop fusion | flops 1769472 | bytes 5898240 | tf_op jit(solution)/shard_map/mul | solution.py:84
  269.3 11.6 %all-to-all-done.3 = bf16[16,64,768]{2,1,0:T(8,128)(2,1)S(1)} async-done(((bf16[16,64,768]{2,1,0:T(8,128)(2,1)}), bf16[16,64,768]{2,1,0:T(8,128)(2,1)S(1)}, u32[]{:S(2)}, u32[]{:S(2)}) %all-to-all-start.3) | async-done | bytes 1572896 | tf_op jit(solution)/shard_map/all_to_all | solution.py:43
  281.1 4.3 %collective-permute-start.5 = (bf16[64,384]{1,0:T(8,128)(2,1)S(1)}, bf16[64,384]{1,0:T(8,128)(2,1)S(1)}, u32[]{:S(2)}, u32[]{:S(2)}) collective-permute-start(bf16[64,384]{1,0:T(8,128)(2,1)S(1)} %slice.37), channel_id=1, source_target_pairs={{0,16},{16,0},{32,48},{48,32},{64,80},{80,64},{96,112},{112,96},{1... | collective-permute-start | bytes 147464 | tf_op jit(solution)/shard_map/ppermute | solution.py:28
  (57 shorter events, 21.4 us)
Async XLA Ops:
  8.0 4.2 %collective-permute-start = (bf16[64,384]{1,0:T(8,128)(2,1)S(1)}, bf16[64,384]{1,0:T(8,128)(2,1)S(1)}, u32[]{:S(2)}, u32[]{:S(2)}) collective-permute-start(bf16[64,384]{1,0:T(8,128)(2,1)S(1)} %get-tuple-element.13), channel_id=1, source_target_pairs={{0,16},{16,0},{32,48},{48,32},{64,80},{80,64},{96,112},{112,96},{1... | collective-permute-start | bytes 147464 | tf_op jit(solution)/shard_map/ppermute | solution.py:28
  12.2 6.4 %copy-start.5 = (bf16[384,1536]{1,0:T(8,128)(2,1)S(1)}, bf16[384,1536]{1,0:T(8,128)(2,1)}, u32[]{:S(2)}) copy-start(bf16[384,1536]{1,0:T(8,128)(2,1)} %param.5) | copy-start | bytes 3538948
  13.6 27.4 %all-to-all-start = ((bf16[16,64,768]{2,1,0:T(8,128)(2,1)}), bf16[16,64,768]{2,1,0:T(8,128)(2,1)S(1)}, u32[]{:S(2)}, u32[]{:S(2)}) async-start(bf16[16,64,768]{2,1,0:T(8,128)(2,1)} %broadcast_in_dim.4), calls=%async_computation | async-start | bytes 3145728 | tf_op jit(solution)/shard_map/all_to_all | solution.py:36
  18.6 73.8 %reduce-scatter.3.cloned.1.call-start = ((), (), s32[]{:S(2)}) async-start(), calls=%async_computation.6 | async-start | bytes 3538944 | tf_op jit(solution)/shard_map/reduce_scatter | solution.py:52
  18.6 3.2 %collective-permute-start.1 = (bf16[384,1536]{1,0:T(8,128)(2,1)S(1)}, bf16[384,1536]{1,0:T(8,128)(2,1)S(1)}, u32[]{:S(2)}, u32[]{:S(2)}) collective-permute-start(bf16[384,1536]{1,0:T(8,128)(2,1)S(1)} %copy-done.5), channel_id=1, source_target_pairs={{0,16},{16,0},{32,48},{48,32},{64,80},{80,64},{96,112},{112,96},{1... | collective-permute-start | bytes 3538952 | tf_op jit(solution)/shard_map/ppermute | solution.py:28
  46.6 0.9 copy-start.6
  47.5 3.6 %collective-permute-start.4 = (bf16[64,384]{1,0:T(8,128)(2,1)S(1)}, bf16[64,384]{1,0:T(8,128)(2,1)S(1)}, u32[]{:S(2)}, u32[]{:S(2)}) collective-permute-start(bf16[64,384]{1,0:T(8,128)(2,1)S(1)} %get-tuple-element.11), channel_id=1, source_target_pairs={{0,16},{16,0},{32,48},{48,32},{64,80},{80,64},{96,112},{112,96},{1... | collective-permute-start | bytes 147464 | tf_op jit(solution)/shard_map/ppermute | solution.py:28
  52.4 27.3 %all-to-all-start.2 = ((bf16[16,64,768]{2,1,0:T(8,128)(2,1)}), bf16[16,64,768]{2,1,0:T(8,128)(2,1)S(1)}, u32[]{:S(2)}, u32[]{:S(2)}) async-start(bf16[16,64,768]{2,1,0:T(8,128)(2,1)} %broadcast_in_dim.5), calls=%async_computation.3 | async-start | bytes 3145728 | tf_op jit(solution)/shard_map/all_to_all | solution.py:36
  56.1 84.9 %reduce-scatter.5.cloned.1.call-start = ((), (), s32[]{:S(2)}) async-start(), calls=%async_computation.8 | async-start | bytes 3538944 | tf_op jit(solution)/shard_map/reduce_scatter | solution.py:52
  56.2 3.1 %collective-permute-start.2 = (bf16[1536,384]{1,0:T(8,128)(2,1)}, bf16[1536,384]{1,0:T(8,128)(2,1)S(1)}, u32[]{:S(2)}, u32[]{:S(2)}) collective-permute-start(bf16[1536,384]{1,0:T(8,128)(2,1)} %param.6), channel_id=1, source_target_pairs={{0,16},{16,0},{32,48},{48,32},{64,80},{80,64},{96,112},{112,96},{1... | collective-permute-start | bytes 3538952 | tf_op jit(solution)/shard_map/ppermute | solution.py:28
  79.8 6.3 %copy-start.3 = (bf16[16,64,768]{2,1,0:T(8,128)(2,1)}, bf16[16,64,768]{2,1,0:T(8,128)(2,1)S(1)}, u32[]{:S(2)}) copy-start(bf16[16,64,768]{2,1,0:T(8,128)(2,1)S(1)} %all-to-all-done.2) | copy-start | bytes 4718596
  86.1 104.4 %all-gather.3.cloned.1.call-start = ((), (), s32[]{:S(2)}) async-start(), calls=%async_computation.7 | async-start | bytes 3538944 | tf_op jit(solution)/shard_map/all_gather | solution.py:58
  143.5 92.2 %all-gather.5.cloned.1.call-start = ((), (), s32[]{:S(2)}) async-start(), calls=%async_computation.9 | async-start | bytes 3538944 | tf_op jit(solution)/shard_map/all_gather | solution.py:58
  196.9 56.9 %all-to-all-start.1 = ((bf16[16,64,768]{2,1,0:T(8,128)(2,1)}), bf16[16,64,768]{2,1,0:T(8,128)(2,1)S(1)}, u32[]{:S(2)}, u32[]{:S(2)}) async-start(bf16[16,64,768]{2,1,0:T(8,128)(2,1)} %bitcast.21), calls=%async_computation.2 | async-start | bytes 3145728 | tf_op jit(solution)/shard_map/all_to_all | solution.py:43
  235.8 6.8 %copy-start.7 = (bf16[1024,1536]{1,0:T(8,128)(2,1)S(1)}, bf16[1024,1536]{1,0:T(8,128)(2,1)}, u32[]{:S(2)}) copy-start(bf16[1024,1536]{1,0:T(8,128)(2,1)} %all-gather.3.cloned.1.call-done) | copy-start | bytes 9437188
  240.5 5.3 %copy-start = (f32[768,1536]{1,0:T(8,128)}, f32[768,1536]{1,0:T(8,128)S(1)}, u32[]{:S(2)}) copy-start(f32[768,1536]{1,0:T(8,128)S(1)} %fusion.11) | copy-start | bytes 14155780
  240.5 2.5 copy-start.4
  241.6 18.7 %collective-permute-start.6 = (bf16[384,1536]{1,0:T(8,128)(2,1)}, bf16[384,1536]{1,0:T(8,128)(2,1)}, u32[]{:S(2)}, u32[]{:S(2)}) collective-permute-start(bf16[384,1536]{1,0:T(8,128)(2,1)} %slice.55), channel_id=1, source_target_pairs={{0,16},{16,0},{32,48},{48,32},{64,80},{80,64},{96,112},{112,96},{1... | collective-permute-start | bytes 3538952 | tf_op jit(solution)/shard_map/ppermute | solution.py:28
  243.0 5.3 %copy-start.1 = (bf16[1024,1536]{1,0:T(8,128)(2,1)S(1)}, bf16[1024,1536]{1,0:T(8,128)(2,1)}, u32[]{:S(2)}) copy-start(bf16[1024,1536]{1,0:T(8,128)(2,1)} %all-gather.5.cloned.1.call-done) | copy-start | bytes 9437188
  245.8 2.5 copy-start.2
  247.1 18.5 %collective-permute-start.7 = (bf16[1536,384]{1,0:T(8,128)(2,1)}, bf16[1536,384]{1,0:T(8,128)(2,1)}, u32[]{:S(2)}, u32[]{:S(2)}) collective-permute-start(bf16[1536,384]{1,0:T(8,128)(2,1)} %slice.54), channel_id=1, source_target_pairs={{0,16},{16,0},{32,48},{48,32},{64,80},{80,64},{96,112},{112,96},{1... | collective-permute-start | bytes 3538952 | tf_op jit(solution)/shard_map/ppermute | solution.py:28
  253.8 27.1 %all-to-all-start.3 = ((bf16[16,64,768]{2,1,0:T(8,128)(2,1)}), bf16[16,64,768]{2,1,0:T(8,128)(2,1)S(1)}, u32[]{:S(2)}, u32[]{:S(2)}) async-start(bf16[16,64,768]{2,1,0:T(8,128)(2,1)} %bitcast.20), calls=%async_computation.5 | async-start | bytes 3145728 | tf_op jit(solution)/shard_map/all_to_all | solution.py:43
  264.4 21.0 %collective-permute-start.3 = (bf16[64,384]{1,0:T(8,128)(2,1)S(1)}, bf16[64,384]{1,0:T(8,128)(2,1)S(1)}, u32[]{:S(2)}, u32[]{:S(2)}) collective-permute-start(bf16[64,384]{1,0:T(8,128)(2,1)S(1)} %slice.35), channel_id=1, source_target_pairs={{0,16},{16,0},{32,48},{48,32},{64,80},{80,64},{96,112},{112,96},{1... | collective-permute-start | bytes 147464 | tf_op jit(solution)/shard_map/ppermute | solution.py:28
  281.1 5.2 %collective-permute-start.5 = (bf16[64,384]{1,0:T(8,128)(2,1)S(1)}, bf16[64,384]{1,0:T(8,128)(2,1)S(1)}, u32[]{:S(2)}, u32[]{:S(2)}) collective-permute-start(bf16[64,384]{1,0:T(8,128)(2,1)S(1)} %slice.37), channel_id=1, source_target_pairs={{0,16},{16,0},{32,48},{48,32},{64,80},{80,64},{96,112},{112,96},{1... | collective-permute-start | bytes 147464 | tf_op jit(solution)/shard_map/ppermute | solution.py:28
Sparse Core Ops, SparseCore 0:
  46.7 45.6 reduce-scatter.2
  94.9 46.0 reduce-scatter.4
  143.7 46.7 all-gather.2
  192.1 43.5 all-gather.4
